TPU v7x, 32 devices: a whole 2x2x4 slice. The times are simulated.
32 devices in a mesh: blk: 8 (over z, x), lab: 4 (over y, core).
Axes of the slice: x: 2, y: 2, z: 4, core: 2. Of those that a mesh axis runs over, the one named last changes fastest.
Arguments:
- features: bfloat16 [4096, 768], P(('blk', 'lab')), may hold values from -0.21875 to 0.21875
- direction: bfloat16 [4, 128, 768], P('lab', 'blk'), may hold values from -6 to 6
- active: int32 [4096, 512], P('blk', 'lab'), may hold values 0 or 1
- shortlist: int32 [32, 4], P('blk', 'lab'), may hold values 0 or 1
Outputs:
- hess_product: float32 [4, 128, 768], P('lab', 'blk')
- curvature: float32 [4, 128], P('lab', 'blk')
All inputs are finite; a program needn't handle non-finite values. No bound on the sum of `active` or of `shortlist` on one device may be relied on, other than what follows from the above.
Results may differ from a plain program's by a relative error of at most 0.00059.
Values may be sent and summed in bfloat16 or wider, within the bound.
A program may use at most 64 MiB of HBM per device.

v0:
```python
import jax
import jax.numpy as jnp
from jax import lax
from jax.sharding import PartitionSpec as P

D = 768
TILE = 128


def active_weights(active, shortlist):
    row_tiles, label_tiles = shortlist.shape
    blocks = active.reshape(row_tiles, TILE, label_tiles, TILE) * shortlist[:, None, :, None]
    return blocks.reshape(active.shape).astype(jnp.bfloat16)


def shards(features, direction, active, shortlist):
    vectors = direction[0]
    gathered = lax.all_gather(vectors, "blk", axis=0, tiled=True)
    weights = active_weights(active, shortlist)
    slab_part = lax.all_gather(features, "lab", axis=0, tiled=True)
    margins = lax.dot_general(
        slab_part, gathered, (((1,), (1,)), ((), ())), preferred_element_type=jnp.float32
    )
    scaled = (weights.astype(jnp.float32) * margins).astype(jnp.bfloat16)
    label_sums = lax.dot_general(
        scaled, slab_part, (((0,), (0,)), ((), ())), preferred_element_type=jnp.float32
    )
    own_total = lax.psum_scatter(label_sums, "blk", scatter_dimension=0, tiled=True)
    product = vectors.astype(jnp.float32) + own_total
    curve = jnp.sum(vectors.astype(jnp.float32) * product, axis=-1) / D
    return (product[None], curve[None])


def solution(mesh):
    return jax.shard_map(
        shards,
        mesh=mesh,
        in_specs=(P(("blk", "lab"), None), P("lab", "blk", None), P("blk", "lab"), P("blk", "lab")),
        out_specs=(P("lab", "blk", None), P("lab", "blk")),
        check_vma=False,
    )
```

profile of v0, /device:TPU:0, one launch (start us, length us, event | category | flops | bytes accessed | tf_op | source)
XLA Modules:
  0.0 121.3 jit_solution(10301555255092412256)
XLA Ops:
  7.2 0.0 copy-start
  7.2 0.0 copy-start.2
  7.2 0.0 reduce-scatter.2.cloned.1.call-start
  7.2 0.6 copy-done
  7.8 0.1 broadcast_bitcast_fusion
  7.9 32.2 %all-gather = bf16[1,128,768]{2,1,0:T(8,128)(2,1)S(1)} all-gather(bf16[1,16,768]{2,1,0:T(8,128)(2,1)} %param.5), channel_id=2, replica_groups=mesh['blk'=8,'lab'=4] {'blk'}, dimensions={1}, use_global_device_ids=true | all-gather | bytes 221184 | tf_op jit(solution)/shard_map/all_gather | solution.py:18
  40.1 0.0 copy-done.2
  40.1 0.0 copy-start.1
  40.1 9.2 %all_gather.6 = bf16[512,768]{1,0:T(8,128)(2,1)S(1)} all-gather(bf16[128,768]{1,0:T(8,128)(2,1)S(1)} %copy-done.2), channel_id=1, replica_groups=mesh['blk'=8,'lab'=4] {'lab'}, dimensions={0}, use_global_device_ids=true | all-gather | bytes 983040 | tf_op jit(solution)/shard_map/all_gather | solution.py:20
  49.3 0.0 copy-done.1
  49.3 1.5 %fusion.1 = f32[128,768]{1,0:T(8,128)} fusion(bf16[512,768]{1,0:T(8,128)(2,1)S(1)} %all_gather.6, bf16[1,128,768]{2,1,0:T(8,128)(2,1)S(1)} %all-gather, s32[512,128]{1,0:T(8,128)S(1)} %copy-done.1, s32[512]{0:T(512)S(1)} %broadcast_bitcast_fusion), kind=kOutput, calls=%fused_computation.2 | convolution fusion | flops 201654272 | bytes 1640448 | tf_op jit(solution)/shard_map/dot_general | solution.py:25
  50.8 0.0 copy-start.3
  50.8 0.0 reduce-scatter.2.cloned.1.call-update
  50.8 61.6 %reduce-scatter.2.cloned.1.call-done = f32[16,768]{1,0:T(8,128)} async-done(((f32[128,768]{1,0:T(8,128)}), f32[16,768]{1,0:T(8,128)}) %reduce-scatter.2.cloned.1.call-update) | async-done | bytes 49168 | tf_op jit(solution)/shard_map/reduce_scatter | solution.py:28
  112.4 0.0 copy-done.3
  112.4 1.5 %fusion.6 = (f32[16]{0:T(128)S(1)}, f32[1,16,768]{2,1,0:T(8,128)}) fusion(f32[16,768]{1,0:T(8,128)} %reduce-scatter.2.cloned.1.call-done, bf16[1,16,768]{2,1,0:T(8,128)(2,1)S(1)} %copy-done.3), kind=kLoop, calls=%fused_computation.9 | loop fusion | flops 49136 | bytes 122944 | tf_op jit(solution)/shard_map/reduce_sum | solution.py:30
  113.9 0.5 multiply_bitcast_fusion
Async XLA Ops:
  7.2 0.7 copy-start
  7.2 32.9 %copy-start.2 = (bf16[128,768]{1,0:T(8,128)(2,1)S(1)}, bf16[128,768]{1,0:T(8,128)(2,1)}, u32[]{:S(2)}) copy-start(bf16[128,768]{1,0:T(8,128)(2,1)} %param.4) | copy-start | bytes 589828
  7.2 105.2 %reduce-scatter.2.cloned.1.call-start = ((), (), s32[]{:S(2)}) async-start(), calls=%async_computation.1 | async-start | bytes 442368 | tf_op jit(solution)/shard_map/reduce_scatter | solution.py:28
  40.1 9.2 %copy-start.1 = (s32[512,128]{1,0:T(8,128)S(1)}, s32[512,128]{1,0:T(8,128)}, u32[]{:S(2)}) copy-start(s32[512,128]{1,0:T(8,128)} %param.6) | copy-start | bytes 786436
  50.8 61.6 %copy-start.3 = (bf16[1,16,768]{2,1,0:T(8,128)(2,1)S(1)}, bf16[1,16,768]{2,1,0:T(8,128)(2,1)}, u32[]{:S(2)}) copy-start(bf16[1,16,768]{2,1,0:T(8,128)(2,1)} %param.5) | copy-start | bytes 73732
Sparse Core Ops, SparseCore 0:
  50.9 61.3 reduce-scatter.1
where the time goes:
time: 121 us
  waiting for transfers between devices  61.6 us (51%)
  blocking collectives  41.4 us (34%)
  between operations  14 us (12%)
  other arithmetic  2.05 us (2%)
  matrix products  1.51 us (1%)
    reduce_scatter x1, waiting for transfers between devices, shards(): lax.psum_scatter(label_sums, 'blk', scatter_dimension=0, tiled=True)  61.6 us
    all_gather x1, blocking collectives, shards(): gathered = lax.all_gather(vectors, 'blk', axis=0, tiled=True)  32.2 us
    all_gather x1, blocking collectives, shards(): slab_part = lax.all_gather(features, 'lab', axis=0, tiled=True)  9.2 us
  transfers between devices with their start and end apart: 1, of which 1 were waited for; matrix products, arithmetic and copies ran while one was open for 0% of the time, Pallas kernels for 0%

commit v1 on v0

v1 whole, which is shorter than its diff:
```python
import functools

import jax
import jax.numpy as jnp
from jax import lax
from jax.experimental import pallas as pl
from jax.experimental.pallas import tpu as pltpu
from jax.sharding import PartitionSpec as P

MESH = pl.DeviceIdType.MESH
CHUNKS = 2


def remote(src, dst, send, recv, **where):
    return pltpu.make_async_remote_copy(
        src_ref=src, dst_ref=dst, send_sem=send, recv_sem=recv, device_id=where, device_id_type=MESH
    )


def kernel(
    n_blk, n_lab, feats, dirs, active, short, hess, curve,
    slab, group, act, weights, scaled, acc, from_x, from_z,
    local_sem, y_send, y_recv, s_send, s_recv, f_send, f_recv,
    g_send, g_recv, x_send, x_recv, z_send, z_recv,
):
    rows, depth = feats.shape
    own = dirs.shape[1]
    n_z, n_pair = n_blk // 2, n_lab // 2
    labels = n_blk * own
    part = rows // CHUNKS
    blk, lab = lax.axis_index("blk"), lax.axis_index("lab")
    x, z = lax.rem(blk, 2), lax.div(blk, 2)
    core, pair = lax.rem(lab, 2), lax.div(lab, 2)
    x_peer = blk + 1 - 2 * x
    core_peer = lab + 1 - 2 * core

    local = [
        pltpu.make_async_copy(feats, slab.at[pair, core], local_sem.at[0]),
        pltpu.make_async_copy(dirs.at[0], group.at[x, z], local_sem.at[1]),
        pltpu.make_async_copy(active, act, local_sem.at[2]),
    ]
    for copy in local:
        copy.start()

    barrier = pltpu.get_barrier_semaphore()
    for k in range(1, n_blk):
        pl.semaphore_signal(barrier, inc=1, device_id={"blk": lax.rem(blk + k, n_blk)}, device_id_type=MESH)
    for k in range(1, n_pair):
        pl.semaphore_signal(
            barrier, inc=1, device_id={"lab": 2 * lax.rem(pair + k, n_pair) + core}, device_id_type=MESH
        )
    pl.semaphore_signal(barrier, inc=1, device_id={"lab": core_peer}, device_id_type=MESH)
    pl.semaphore_wait(barrier, n_blk - 1 + n_pair)

    sent = []

    def go(copy):
        copy.start()
        sent.append(copy)

    for c in range(CHUNKS):
        piece = pl.ds(c * part, part)
        for k in range(1, n_pair):
            go(remote(
                feats.at[piece], slab.at[pair, core, piece], y_send.at[k - 1, c], y_recv.at[k - 1, c],
                lab=2 * lax.rem(pair + k, n_pair) + core,
            ))
    for k in range(1, n_blk):
        go(remote(
            dirs.at[0], group.at[x, z], g_send.at[k - 1], g_recv.at[k - 1], blk=lax.rem(blk + k, n_blk)
        ))
    go(remote(feats, slab.at[pair, core], s_send.at[0], s_recv.at[0], lab=core_peer))

    local[2].wait()
    row_tile = active.shape[0] // short.shape[0]
    label_tile = active.shape[1] // short.shape[1]
    for r in range(short.shape[0]):
        for t in range(short.shape[1]):
            tile = act[r * row_tile:(r + 1) * row_tile, t * label_tile:(t + 1) * label_tile] * short[r, t]
            tile = tile.astype(jnp.float32).T
            at_pair, offset = divmod(r * row_tile, 2 * rows)
            for j in range(label_tile // own):
                device = t * (label_tile // own) + j
                slot = (device % 2) * n_z * own + (device // 2) * own
                weights[at_pair, slot:slot + own, offset:offset + row_tile] = tile[j * own:(j + 1) * own]

    for k in range(1, n_pair):
        source = lax.rem(pair + n_pair - k, n_pair)
        for c in range(CHUNKS):
            piece = pl.ds(c * part, part)
            block = slab.at[source, core, piece]
            remote(block, block, y_send.at[k - 1, c], y_recv.at[k - 1, c], lab=core_peer).wait_recv()
            go(remote(block, block, f_send.at[k - 1, c], f_recv.at[k - 1, c], lab=core_peer))

    local[0].wait()
    local[1].wait()
    other = slab.at[pair, 1 - core]
    remote(other, other, s_send.at[0], s_recv.at[0], lab=core_peer).wait_recv()
    for k in range(1, n_blk):
        source = lax.rem(blk + n_blk - k, n_blk)
        block = group.at[lax.rem(source, 2), lax.div(source, 2)]
        remote(block, block, g_send.at[k - 1], g_recv.at[k - 1], blk=x_peer).wait_recv()

    def masked(at):
        margins = lax.dot_general(
            group[...].reshape(labels, depth), slab[at].reshape(2 * rows, depth),
            (((1,), (1,)), ((), ())), preferred_element_type=jnp.float32,
        )
        return (weights[at] * margins).astype(jnp.bfloat16)

    def arrive(k):
        source = lax.rem(pair + n_pair - k, n_pair)
        for c in range(CHUNKS):
            block = slab.at[source, 1 - core, pl.ds(c * part, part)]
            remote(block, block, f_send.at[k - 1, c], f_recv.at[k - 1, c], lab=core_peer).wait_recv()
        return source

    def whole(at):
        return jnp.dot(
            masked(at), slab[at].reshape(2 * rows, depth), preferred_element_type=jnp.float32
        ).reshape(acc.shape)

    acc[...] = whole(pair)
    if n_pair > 2:
        @pl.loop(1, n_pair - 1)
        def _(k):
            acc[...] += whole(arrive(k))

    last = arrive(n_pair - 1)
    scaled[...] = masked(last).reshape(scaled.shape)

    def finish(half):
        acc[half] += jnp.dot(
            scaled[half], slab[last].reshape(2 * rows, depth), preferred_element_type=jnp.float32
        ).reshape(acc.shape[1:])

    finish(1 - x)
    for i in range(n_z):
        to = lax.rem(z + 1 + i, n_z)
        go(remote(acc.at[1 - x, to], from_x.at[to], x_send.at[i], x_recv.at[i], blk=x_peer))
    finish(x)
    for i in range(n_z):
        to = lax.rem(z + 1 + i, n_z)
        block = from_x.at[to]
        remote(block, block, x_send.at[i], x_recv.at[i], blk=x_peer).wait_recv()
        acc[x, to] += from_x[to]
        if i < n_z - 1:
            go(remote(acc.at[x, to], from_z.at[i], z_send.at[i], z_recv.at[i], blk=2 * to + x))

    vectors = group[x, z].astype(jnp.float32)
    total = acc[x, z]
    for i in range(n_z - 1):
        block = from_z.at[i]
        remote(block, block, z_send.at[i], z_recv.at[i], blk=x_peer).wait_recv()
        total += from_z[i]
    product = vectors + total
    hess[0] = product
    column = jnp.sum(vectors * product, axis=1, keepdims=True) / depth
    at_row = lax.broadcasted_iota(jnp.int32, (own, own), 0)
    at_column = lax.broadcasted_iota(jnp.int32, (own, own), 1)
    curve[...] = jnp.sum(jnp.where(at_row == at_column, column, 0.0), axis=0, keepdims=True)

    for copy in sent:
        copy.wait_send()


def solution(mesh):
    n_blk, n_lab = mesh.shape["blk"], mesh.shape["lab"]

    def shards(features, direction, active, shortlist):
        rows, depth = features.shape
        own = direction.shape[1]
        n_z, n_pair = n_blk // 2, n_lab // 2
        labels = n_blk * own
        dma = pltpu.SemaphoreType.DMA
        others = max(n_pair - 1, 1)
        scratch = [
            pltpu.VMEM((n_pair, 2, rows, depth), features.dtype),
            pltpu.VMEM((2, n_z, own, depth), direction.dtype),
            pltpu.VMEM(active.shape, active.dtype),
            pltpu.VMEM((n_pair, labels, 2 * rows), jnp.float32),
            pltpu.VMEM((2, n_z * own, 2 * rows), jnp.bfloat16),
            pltpu.VMEM((2, n_z, own, depth), jnp.float32),
            pltpu.VMEM((n_z, own, depth), jnp.float32),
            pltpu.VMEM((n_z - 1, own, depth), jnp.float32),
            dma((3,)),
            dma((others, CHUNKS)), dma((others, CHUNKS)),
            dma((1,)), dma((1,)),
            dma((others, CHUNKS)), dma((others, CHUNKS)),
            dma((n_blk - 1,)), dma((n_blk - 1,)),
            dma((n_z,)), dma((n_z,)),
            dma((n_z - 1,)), dma((n_z - 1,)),
        ]
        held = sum(
            functools.reduce(lambda a, b: a * b, s.shape) * jnp.dtype(s.dtype).itemsize for s in scratch[:8]
        )
        anywhere = pl.BlockSpec(memory_space=pl.ANY)
        vmem = pl.BlockSpec(memory_space=pltpu.VMEM)
        return pl.pallas_call(
            functools.partial(kernel, n_blk, n_lab),
            out_shape=(
                jax.ShapeDtypeStruct((1, own, depth), jnp.float32),
                jax.ShapeDtypeStruct((1, own), jnp.float32),
            ),
            in_specs=[anywhere, anywhere, anywhere, pl.BlockSpec(memory_space=pltpu.SMEM)],
            out_specs=(vmem, vmem),
            scratch_shapes=scratch,
            compiler_params=pltpu.CompilerParams(
                collective_id=0, has_side_effects=True, vmem_limit_bytes=2 * held + (8 << 20)
            ),
            name="hessian",
        )(features, direction, active, shortlist)

    return jax.shard_map(
        shards,
        mesh=mesh,
        in_specs=(P(("blk", "lab"), None), P("lab", "blk", None), P("blk", "lab"), P("blk", "lab")),
        out_specs=(P("lab", "blk", None), P("lab", "blk")),
        check_vma=False,
    )
```

time: 121 us -> 28.6 us (0.24)
  waiting for transfers between devices: 61.6 us -> 0 us
  blocking collectives: 41.4 us -> 0 us
  Pallas kernels: 0 us -> 23.2 us
  between operations: 14 us -> 0.64 us
  local copies, waits for them, and re-layouts: 0.68 us -> 4.49 us
  other arithmetic: 2.05 us -> 0 us
  matrix products: 1.51 us -> 0 us
    reduce_scatter x1 -> x0, waiting for transfers between devices: 61.6 us -> none  [shards(): lax.psum_scatter(label_sums, 'blk', scatter_dimension=0, tiled=True)]
    all_gather x2 -> x0, blocking collectives: 41.4 us -> none  [the longest x1 32.2 us: shards(): gathered = lax.all_gather(vectors, 'blk', axis=0, tiled=True)]
    pallas_call x0 -> x1, Pallas kernels: none -> 23.2 us  [shards(): pl.pallas_call(functools.partial(kernel, n_blk, n_lab), out_shape=(jax.Sh...]
    unnamed x8 -> x9, local copies, waits for them, and re-layouts: 0.61 us -> 4.49 us
    reduce_sum x1 -> x0, other arithmetic: 1.54 us -> none  [shards(): curve = jnp.sum(vectors.astype(jnp.float32) * product, axis=-1) / D]
    dot_general x1 -> x0, matrix products: 1.51 us -> none  [shards(): lax.dot_general(scaled, slab_part, (((0,), (0,)), ((), ())), preferred_el...]
  transfers between devices with their start and end apart: 1 -> 0, of which waited for: 1 -> 0; matrix products, arithmetic and copies ran while one was open for 0% -> 0% of each run, Pallas kernels for 0% -> 0%
where the time goes in v1:
time: 28.6 us; the launch traced here: 28.3 us
  Pallas kernels  23.2 us (81%)
  local copies, waits for them, and re-layouts  4.49 us (16%)
  between operations  0.64 us (2%)
    pallas_call x1, Pallas kernels, shards(): pl.pallas_call(functools.partial(kernel, n_blk, n_lab), out_shape=(jax.Sh...  23.2 us
    unnamed x9, local copies, waits for them, and re-layouts  4.49 us

profile of v1, /device:TPU:0, one launch (start us, length us, event | category | flops | bytes accessed | tf_op | source)
XLA Modules:
  0.0 28.3 jit_solution(9113651852419859902)
XLA Ops:
  0.6 0.7 %copy.6.short = s32[4,1]{1,0:T(4,128)S(1)} copy(s32[4,1]{0,1:T(1,128)} %param.7) | data formatting | bytes 32 | tf_op args[3]
  1.4 0.0 copy-start
  1.4 0.9 %copy-done = s32[512,128]{1,0:T(8,128)S(1)} copy-done((s32[512,128]{1,0:T(8,128)S(1)}, s32[512,128]{1,0:T(8,128)}, u32[]{:S(2)}) %copy-start) | copy-done | bytes 262168
  2.3 0.0 copy-start.1
  2.3 0.9 %copy-done.1 = bf16[128,768]{1,0:T(8,128)(2,1)S(1)} copy-done((bf16[128,768]{1,0:T(8,128)(2,1)S(1)}, bf16[128,768]{1,0:T(8,128)(2,1)}, u32[]{:S(2)}) %copy-start.1) | copy-done | bytes 196632
  3.2 0.0 copy-start.2
  3.3 0.7 %copy-done.2 = bf16[1,16,768]{2,1,0:T(8,128)(2,1)S(1)} copy-done((bf16[1,16,768]{2,1,0:T(8,128)(2,1)S(1)}, bf16[1,16,768]{2,1,0:T(8,128)(2,1)}, u32[]{:S(2)}) %copy-start.2) | copy-done | bytes 24600
  4.0 23.2 %hessian.1 = (f32[1,16,768]{2,1,0:T(8,128)S(1)}, f32[1,16]{1,0:T(1,128)S(1)}) custom-call(bf16[128,768]{1,0:T(8,128)(2,1)S(1)} %copy-done.1, bf16[1,16,768]{2,1,0:T(8,128)(2,1)S(1)} %copy-done.2, s32[512,128]{1,0:T(8,128)S(1)} %copy-done, s32[4,1]{1,0:T(4,128)S(1)} %copy.6.short), custom_call_target="tpu_custom_call" | custom-call | tf_op jit(solution)/shard_map/hessian/pallas_call | solution.py:199
  27.2 0.6 %copy.9 = f32[1,16,768]{2,1,0:T(8,128)} copy(f32[1,16,768]{2,1,0:T(8,128)S(1)} %get-tuple-element.4) | data formatting | bytes 98304
  27.8 0.5 %copy.10 = f32[1,16]{1,0:T(1,128)} copy(f32[1,16]{1,0:T(1,128)S(1)} %get-tuple-element.5) | data formatting | bytes 128
Async XLA Ops:
  1.4 0.9 %copy-start = (s32[512,128]{1,0:T(8,128)S(1)}, s32[512,128]{1,0:T(8,128)}, u32[]{:S(2)}) copy-start(s32[512,128]{1,0:T(8,128)} %active.1) | copy-start | bytes 786436
  2.3 0.9 %copy-start.1 = (bf16[128,768]{1,0:T(8,128)(2,1)S(1)}, bf16[128,768]{1,0:T(8,128)(2,1)}, u32[]{:S(2)}) copy-start(bf16[128,768]{1,0:T(8,128)(2,1)} %feats.1) | copy-start | bytes 589828
  3.2 0.7 %copy-start.2 = (bf16[1,16,768]{2,1,0:T(8,128)(2,1)S(1)}, bf16[1,16,768]{2,1,0:T(8,128)(2,1)}, u32[]{:S(2)}) copy-start(bf16[1,16,768]{2,1,0:T(8,128)(2,1)} %dirs.1) | copy-start | bytes 73732

commit v2 on v1

v2 whole, which is shorter than its diff:
```python
import functools

import jax
import jax.numpy as jnp
from jax import lax
from jax.experimental import pallas as pl
from jax.experimental.pallas import tpu as pltpu
from jax.sharding import PartitionSpec as P

MESH = pl.DeviceIdType.MESH
CHUNKS = 2
PIECES = 2


def remote(src, dst, send, recv, **where):
    return pltpu.make_async_remote_copy(
        src_ref=src, dst_ref=dst, send_sem=send, recv_sem=recv, device_id=where, device_id_type=MESH
    )


def kernel(
    n_blk, n_lab, feats, dirs, active, short, hess,
    slab, group, act, tiles, weights, scaled, acc, from_x, from_z,
    local_sem, y_send, y_recv, s_send, s_recv, f_send, f_recv,
    g_send, g_recv, h_send, h_recv, x_send, x_recv, z_send, z_recv,
):
    rows, depth = feats.shape
    own = dirs.shape[1]
    n_z, n_pair = n_blk // 2, n_lab // 2
    labels = n_blk * own
    part = rows // CHUNKS
    blk, lab = lax.axis_index("blk"), lax.axis_index("lab")
    x, z = lax.rem(blk, 2), lax.div(blk, 2)
    core, pair = lax.rem(lab, 2), lax.div(lab, 2)
    x_peer = blk + 1 - 2 * x
    core_peer = lab + 1 - 2 * core

    local = [
        pltpu.make_async_copy(feats, slab.at[pair, core], local_sem.at[0]),
        pltpu.make_async_copy(dirs.at[0], group.at[x, z], local_sem.at[1]),
        pltpu.make_async_copy(active, act, local_sem.at[2]),
        pltpu.make_async_copy(short, tiles, local_sem.at[3]),
    ]
    for copy in local:
        copy.start()

    barrier = pltpu.get_barrier_semaphore()
    for k in range(1, n_z):
        pl.semaphore_signal(
            barrier, inc=1, device_id={"blk": 2 * lax.rem(z + k, n_z) + x}, device_id_type=MESH
        )
    pl.semaphore_signal(barrier, inc=1, device_id={"blk": x_peer}, device_id_type=MESH)
    for k in range(1, n_pair):
        pl.semaphore_signal(
            barrier, inc=1, device_id={"lab": 2 * lax.rem(pair + k, n_pair) + core}, device_id_type=MESH
        )
    pl.semaphore_signal(barrier, inc=1, device_id={"lab": core_peer}, device_id_type=MESH)
    pl.semaphore_wait(barrier, n_z + n_pair)

    sent = []

    def go(copy):
        copy.start()
        sent.append(copy)

    for c in range(CHUNKS):
        piece = pl.ds(c * part, part)
        for k in range(1, n_pair):
            go(remote(
                feats.at[piece], slab.at[pair, core, piece], y_send.at[k - 1, c], y_recv.at[k - 1, c],
                lab=2 * lax.rem(pair + k, n_pair) + core,
            ))
    for k in range(1, n_z):
        go(remote(
            dirs.at[0], group.at[x, z], g_send.at[k - 1], g_recv.at[k - 1], blk=2 * lax.rem(z + k, n_z) + x
        ))
    go(remote(dirs.at[0], group.at[x, z], h_send.at[0], h_recv.at[0], blk=x_peer))
    go(remote(feats, slab.at[pair, core], s_send.at[0], s_recv.at[0], lab=core_peer))

    local[2].wait()
    local[3].wait()
    row_tile = active.shape[0] // short.shape[1]
    label_tile = active.shape[1] // short.shape[0]
    for r in range(short.shape[1]):
        for t in range(short.shape[0]):
            tile = act[r * row_tile:(r + 1) * row_tile, t * label_tile:(t + 1) * label_tile] * tiles[t:t + 1, r:r + 1]
            tile = tile.astype(jnp.float32).T
            at_pair, offset = divmod(r * row_tile, 2 * rows)
            for j in range(label_tile // own):
                device = t * (label_tile // own) + j
                slot = (device % 2) * n_z * own + (device // 2) * own
                weights[at_pair, slot:slot + own, offset:offset + row_tile] = tile[j * own:(j + 1) * own]

    for k in range(1, n_z):
        block = group.at[x, lax.rem(z + n_z - k, n_z)]
        remote(block, block, g_send.at[k - 1], g_recv.at[k - 1], blk=x_peer).wait_recv()
        go(remote(block, block, h_send.at[k], h_recv.at[k], blk=x_peer))

    def pass_on(c):
        for k in range(1, n_pair):
            block = slab.at[lax.rem(pair + n_pair - k, n_pair), core, pl.ds(c * part, part)]
            remote(block, block, y_send.at[k - 1, c], y_recv.at[k - 1, c], lab=core_peer).wait_recv()
            go(remote(block, block, f_send.at[k - 1, c], f_recv.at[k - 1, c], lab=core_peer))

    for c in range(CHUNKS - 1):
        pass_on(c)
    local[0].wait()
    local[1].wait()
    other = slab.at[pair, 1 - core]
    remote(other, other, s_send.at[0], s_recv.at[0], lab=core_peer).wait_recv()
    for k in range(n_z):
        block = group.at[1 - x, lax.rem(z + n_z - k, n_z)]
        remote(block, block, h_send.at[k], h_recv.at[k], blk=x_peer).wait_recv()

    def masked(at):
        margins = lax.dot_general(
            group[...].reshape(labels, depth), slab[at].reshape(2 * rows, depth),
            (((1,), (1,)), ((), ())), preferred_element_type=jnp.float32,
        )
        return (weights[at] * margins).astype(jnp.bfloat16)

    def arrive(k):
        source = lax.rem(pair + n_pair - k, n_pair)
        for c in range(CHUNKS):
            block = slab.at[source, 1 - core, pl.ds(c * part, part)]
            remote(block, block, f_send.at[k - 1, c], f_recv.at[k - 1, c], lab=core_peer).wait_recv()
        return source

    def whole(at):
        return jnp.dot(
            masked(at), slab[at].reshape(2 * rows, depth), preferred_element_type=jnp.float32
        ).reshape(acc.shape)

    acc[...] = whole(pair)
    pass_on(CHUNKS - 1)
    if n_pair > 2:
        @pl.loop(1, n_pair - 1)
        def _(k):
            acc[...] += whole(arrive(k))

    last = arrive(n_pair - 1)
    scaled[...] = masked(last).reshape(scaled.shape)

    def finish(half):
        acc[half] += jnp.dot(
            scaled[half], slab[last].reshape(2 * rows, depth), preferred_element_type=jnp.float32
        ).reshape(acc.shape[1:])

    finish(1 - x)
    step = own // PIECES
    for i in range(n_z):
        to = lax.rem(z + 1 + i, n_z)
        for c in range(PIECES):
            piece = pl.ds(c * step, step)
            go(remote(
                acc.at[1 - x, to, piece], from_x.at[to, piece], x_send.at[i, c], x_recv.at[i, c], blk=x_peer
            ))
    finish(x)
    for i in range(n_z):
        to = lax.rem(z + 1 + i, n_z)
        for c in range(PIECES):
            piece = pl.ds(c * step, step)
            block = from_x.at[to, piece]
            remote(block, block, x_send.at[i, c], x_recv.at[i, c], blk=x_peer).wait_recv()
            acc[x, to, piece] += from_x[to, piece]
            if i < n_z - 1:
                go(remote(
                    acc.at[x, to, piece], from_z.at[i, piece], z_send.at[i, c], z_recv.at[i, c], blk=2 * to + x
                ))

    vectors = group[x, z].astype(jnp.float32)
    total = acc[x, z]
    for i in range(n_z - 1):
        for c in range(PIECES):
            block = from_z.at[i, pl.ds(c * step, step)]
            remote(block, block, z_send.at[i, c], z_recv.at[i, c], blk=x_peer).wait_recv()
        total += from_z[i]
    product = vectors + total
    hess[0, :own] = product
    column = jnp.sum(vectors * product, axis=1, keepdims=True) / depth
    at_row = lax.broadcasted_iota(jnp.int32, (own, own), 0)
    at_column = lax.broadcasted_iota(jnp.int32, (own, own), 1)
    hess[0, own:own + 1, :own] = jnp.sum(jnp.where(at_row == at_column, column, 0.0), axis=0, keepdims=True)

    for copy in sent:
        copy.wait_send()


def solution(mesh):
    n_blk, n_lab = mesh.shape["blk"], mesh.shape["lab"]

    def shards(features, direction, active, shortlist):
        rows, depth = features.shape
        own = direction.shape[1]
        n_z, n_pair = n_blk // 2, n_lab // 2
        labels = n_blk * own
        dma = pltpu.SemaphoreType.DMA
        others = max(n_pair - 1, 1)
        scratch = [
            pltpu.VMEM((n_pair, 2, rows, depth), features.dtype),
            pltpu.VMEM((2, n_z, own, depth), direction.dtype),
            pltpu.VMEM(active.shape, active.dtype),
            pltpu.VMEM(shortlist.shape[::-1], shortlist.dtype),
            pltpu.VMEM((n_pair, labels, 2 * rows), jnp.float32),
            pltpu.VMEM((2, n_z * own, 2 * rows), jnp.bfloat16),
            pltpu.VMEM((2, n_z, own, depth), jnp.float32),
            pltpu.VMEM((n_z, own, depth), jnp.float32),
            pltpu.VMEM((n_z - 1, own, depth), jnp.float32),
            dma((4,)),
            dma((others, CHUNKS)), dma((others, CHUNKS)),
            dma((1,)), dma((1,)),
            dma((others, CHUNKS)), dma((others, CHUNKS)),
            dma((n_z - 1,)), dma((n_z - 1,)),
            dma((n_z,)), dma((n_z,)),
            dma((n_z, PIECES)), dma((n_z, PIECES)),
            dma((n_z - 1, PIECES)), dma((n_z - 1, PIECES)),
        ]
        hbm = pl.BlockSpec(memory_space=pltpu.HBM)
        vmem = pl.BlockSpec(memory_space=pltpu.VMEM)
        out, = pl.pallas_call(
            functools.partial(kernel, n_blk, n_lab),
            out_shape=(
                jax.ShapeDtypeStruct((1, own + 8, depth), jnp.float32),
            ),
            in_specs=[hbm, hbm, hbm, hbm],
            out_specs=(vmem,),
            scratch_shapes=scratch,
            compiler_params=pltpu.CompilerParams(
                collective_id=0, has_side_effects=True, vmem_limit_bytes=60 << 20
            ),
            name="hessian",
        )(features, direction, active, shortlist.T)
        return out[:, :own], out[:, own, :own]

    return jax.shard_map(
        shards,
        mesh=mesh,
        in_specs=(P(("blk", "lab"), None), P("lab", "blk", None), P("blk", "lab"), P("blk", "lab")),
        out_specs=(P("lab", "blk", None), P("lab", "blk")),
        check_vma=False,
    )
```

time: 28.6 us -> 27.3 us (0.955)
  local copies, waits for them, and re-layouts: 4.49 us -> 2.61 us
  Pallas kernels: 23.2 us -> 23.8 us
    unnamed x9 -> x0, local copies, waits for them, and re-layouts: 4.49 us -> none
    slice x0 -> x1, local copies, waits for them, and re-layouts: none -> 1.42 us  [shards(): return (out[:, :own], out[:, own, :own])]
    squeeze x0 -> x1, local copies, waits for them, and re-layouts: none -> 1.19 us  [shards(): return (out[:, :own], out[:, own, :own])]
    pallas_call x1, Pallas kernels: 23.2 us -> 23.8 us  [shards(): pl.pallas_call(functools.partial(kernel, n_blk, n_lab), out_shape=(jax.Sh...]
where the time goes in v2:
time: 27.3 us; the launch traced here: 27.1 us
  Pallas kernels  23.8 us (87%)
  local copies, waits for them, and re-layouts  2.61 us (10%)
  between operations  0.64 us (2%)
    pallas_call x1, Pallas kernels, shards(): pl.pallas_call(functools.partial(kernel, n_blk, n_lab), out_shape=(jax.Sh...  23.8 us
    slice x1, local copies, waits for them, and re-layouts, shards(): return (out[:, :own], out[:, own, :own])  1.42 us
    squeeze x1, local copies, waits for them, and re-layouts, shards(): return (out[:, :own], out[:, own, :own])  1.19 us

profile of v2, /device:TPU:0, one launch (start us, length us, event | category | flops | bytes accessed | tf_op | source)
XLA Modules:
  0.0 27.1 jit_solution(9736133032302024458)
XLA Ops:
  0.6 23.8 %hessian.1 = f32[1,24,768]{2,1,0:T(8,128)} custom-call(bf16[128,768]{1,0:T(8,128)(2,1)} %feats.1, bf16[1,16,768]{2,1,0:T(8,128)(2,1)} %dirs.1, s32[512,128]{1,0:T(8,128)} %active.1, s32[1,4]{1,0:T(1,128)} %bitcast.3), custom_call_target="tpu_custom_call" | custom-call | tf_op jit(solution)/shard_map/hessian/pallas_call | solution.py:220
  24.4 1.2 %slice_bitcast_fusion = f32[1,16]{1,0:T(1,128)} fusion(f32[1,24,768]{2,1,0:T(8,128)} %hessian.1), kind=kLoop, calls=%fused_computation | loop fusion | bytes 128 | tf_op jit(solution)/shard_map/squeeze | solution.py:233
  25.6 1.4 %slice.6 = f32[1,16,768]{2,1,0:T(8,128)} slice(f32[1,24,768]{2,1,0:T(8,128)} %hessian.1), slice={[0:1], [0:16], [0:768]} | slice | bytes 98304 | tf_op jit(solution)/shard_map/slice | solution.py:233

commit v3 on v2

--- a/solution.py
+++ b/solution.py
@@ -19,7 +19,7 @@
 
 
 def kernel(
-    n_blk, n_lab, feats, dirs, active, short, hess,
+    n_blk, n_lab, feats, dirs, active, short, hess, curve,
     slab, group, act, tiles, weights, scaled, acc, from_x, from_z,
     local_sem, y_send, y_recv, s_send, s_recv, f_send, f_recv,
     g_send, g_recv, h_send, h_recv, x_send, x_recv, z_send, z_recv,
@@ -85,11 +85,11 @@
         for t in range(short.shape[0]):
             tile = act[r * row_tile:(r + 1) * row_tile, t * label_tile:(t + 1) * label_tile] * tiles[t:t + 1, r:r + 1]
             tile = tile.astype(jnp.float32).T
-            at_pair, offset = divmod(r * row_tile, 2 * rows)
+            block, offset = divmod(r * row_tile, rows)
             for j in range(label_tile // own):
                 device = t * (label_tile // own) + j
                 slot = (device % 2) * n_z * own + (device // 2) * own
-                weights[at_pair, slot:slot + own, offset:offset + row_tile] = tile[j * own:(j + 1) * own]
+                weights[block // 2, block % 2, slot:slot + own, offset:offset + row_tile] = tile[j * own:(j + 1) * own]
 
     for k in range(1, n_z):
         block = group.at[x, lax.rem(z + n_z - k, n_z)]
@@ -102,48 +102,52 @@
             remote(block, block, y_send.at[k - 1, c], y_recv.at[k - 1, c], lab=core_peer).wait_recv()
             go(remote(block, block, f_send.at[k - 1, c], f_recv.at[k - 1, c], lab=core_peer))
 
-    for c in range(CHUNKS - 1):
+    for c in range(CHUNKS):
         pass_on(c)
     local[0].wait()
     local[1].wait()
-    other = slab.at[pair, 1 - core]
-    remote(other, other, s_send.at[0], s_recv.at[0], lab=core_peer).wait_recv()
     for k in range(n_z):
         block = group.at[1 - x, lax.rem(z + n_z - k, n_z)]
         remote(block, block, h_send.at[k], h_recv.at[k], blk=x_peer).wait_recv()
 
-    def masked(at):
+    def masked(at, side):
         margins = lax.dot_general(
-            group[...].reshape(labels, depth), slab[at].reshape(2 * rows, depth),
+            group[...].reshape(labels, depth), slab[at, side],
             (((1,), (1,)), ((), ())), preferred_element_type=jnp.float32,
         )
-        return (weights[at] * margins).astype(jnp.bfloat16)
+        return (weights[at, side] * margins).astype(jnp.bfloat16)
+
+    def whole(at, side):
+        return jnp.dot(
+            masked(at, side), slab[at, side], preferred_element_type=jnp.float32
+        ).reshape(acc.shape)
 
     def arrive(k):
         source = lax.rem(pair + n_pair - k, n_pair)
         for c in range(CHUNKS):
             block = slab.at[source, 1 - core, pl.ds(c * part, part)]
             remote(block, block, f_send.at[k - 1, c], f_recv.at[k - 1, c], lab=core_peer).wait_recv()
-        return source
-
-    def whole(at):
-        return jnp.dot(
-            masked(at), slab[at].reshape(2 * rows, depth), preferred_element_type=jnp.float32
-        ).reshape(acc.shape)
-
-    acc[...] = whole(pair)
-    pass_on(CHUNKS - 1)
+
+    acc[...] = whole(pair, core)
+    other = slab.at[pair, 1 - core]
+    remote(other, other, s_send.at[0], s_recv.at[0], lab=core_peer).wait_recv()
+    acc[...] += whole(pair, 1 - core)
     if n_pair > 2:
         @pl.loop(1, n_pair - 1)
         def _(k):
-            acc[...] += whole(arrive(k))
-
-    last = arrive(n_pair - 1)
-    scaled[...] = masked(last).reshape(scaled.shape)
+            source = lax.rem(pair + n_pair - k, n_pair)
+            acc[...] += whole(source, core)
+            arrive(k)
+            acc[...] += whole(source, 1 - core)
+
+    last = lax.rem(pair + 1, n_pair)
+    acc[...] += whole(last, core)
+    arrive(n_pair - 1)
+    scaled[...] = masked(last, 1 - core).reshape(scaled.shape)
 
     def finish(half):
         acc[half] += jnp.dot(
-            scaled[half], slab[last].reshape(2 * rows, depth), preferred_element_type=jnp.float32
+            scaled[half], slab[last, 1 - core], preferred_element_type=jnp.float32
         ).reshape(acc.shape[1:])
 
     finish(1 - x)
@@ -176,11 +180,11 @@
             remote(block, block, z_send.at[i, c], z_recv.at[i, c], blk=x_peer).wait_recv()
         total += from_z[i]
     product = vectors + total
-    hess[0, :own] = product
+    hess[0] = product
     column = jnp.sum(vectors * product, axis=1, keepdims=True) / depth
     at_row = lax.broadcasted_iota(jnp.int32, (own, own), 0)
     at_column = lax.broadcasted_iota(jnp.int32, (own, own), 1)
-    hess[0, own:own + 1, :own] = jnp.sum(jnp.where(at_row == at_column, column, 0.0), axis=0, keepdims=True)
+    curve[...] = jnp.sum(jnp.where(at_row == at_column, column, 0.0), axis=0, keepdims=True)
 
     for copy in sent:
         copy.wait_send()
@@ -201,8 +205,8 @@
             pltpu.VMEM((2, n_z, own, depth), direction.dtype),
             pltpu.VMEM(active.shape, active.dtype),
             pltpu.VMEM(shortlist.shape[::-1], shortlist.dtype),
-            pltpu.VMEM((n_pair, labels, 2 * rows), jnp.float32),
-            pltpu.VMEM((2, n_z * own, 2 * rows), jnp.bfloat16),
+            pltpu.VMEM((n_pair, 2, labels, rows), jnp.float32),
+            pltpu.VMEM((2, n_z * own, rows), jnp.bfloat16),
             pltpu.VMEM((2, n_z, own, depth), jnp.float32),
             pltpu.VMEM((n_z, own, depth), jnp.float32),
             pltpu.VMEM((n_z - 1, own, depth), jnp.float32),
@@ -217,20 +221,20 @@
         ]
         hbm = pl.BlockSpec(memory_space=pltpu.HBM)
         vmem = pl.BlockSpec(memory_space=pltpu.VMEM)
-        out, = pl.pallas_call(
+        return pl.pallas_call(
             functools.partial(kernel, n_blk, n_lab),
             out_shape=(
-                jax.ShapeDtypeStruct((1, own + 8, depth), jnp.float32),
+                pltpu.VMEM((1, own, depth), jnp.float32),
+                pltpu.VMEM((1, own), jnp.float32),
             ),
             in_specs=[hbm, hbm, hbm, hbm],
-            out_specs=(vmem,),
+            out_specs=(vmem, vmem),
             scratch_shapes=scratch,
             compiler_params=pltpu.CompilerParams(
                 collective_id=0, has_side_effects=True, vmem_limit_bytes=60 << 20
             ),
             name="hessian",
         )(features, direction, active, shortlist.T)
-        return out[:, :own], out[:, own, :own]
 
     return jax.shard_map(
         shards,

time: 27.3 us -> 24.4 us (0.89)
  local copies, waits for them, and re-layouts: 2.61 us -> 1.13 us
  Pallas kernels: 23.8 us -> 22.5 us
    slice x1 -> x0, local copies, waits for them, and re-layouts: 1.42 us -> none  [shards(): return (out[:, :own], out[:, own, :own])]
    pallas_call x1, Pallas kernels: 23.8 us -> 22.5 us  [shards(): pl.pallas_call(functools.partial(kernel, n_blk, n_lab), out_shape=(pltpu....]
    squeeze x1 -> x0, local copies, waits for them, and re-layouts: 1.19 us -> none  [shards(): return (out[:, :own], out[:, own, :own])]
    unnamed x0 -> x2, local copies, waits for them, and re-layouts: none -> 1.13 us
where the time goes in v3:
time: 24.4 us; the launch traced here: 24.2 us
  Pallas kernels  22.5 us (92%)
  local copies, waits for them, and re-layouts  1.13 us (5%)
  between operations  0.64 us (3%)
    pallas_call x1, Pallas kernels, shards(): pl.pallas_call(functools.partial(kernel, n_blk, n_lab), out_shape=(pltpu....  22.5 us
    unnamed x2, local copies, waits for them, and re-layouts  1.13 us

profile of v3, /device:TPU:0, one launch (start us, length us, event | category | flops | bytes accessed | tf_op | source)
XLA Modules:
  0.0 24.2 jit_solution(17255688454439836829)
XLA Ops:
  0.6 22.5 %hessian.1 = (f32[1,16,768]{2,1,0:T(8,128)S(1)}, f32[1,16]{1,0:T(1,128)S(1)}) custom-call(bf16[128,768]{1,0:T(8,128)(2,1)} %feats.1, bf16[1,16,768]{2,1,0:T(8,128)(2,1)} %dirs.1, s32[512,128]{1,0:T(8,128)} %active.1, s32[1,4]{1,0:T(1,128)} %bitcast.1), custom_call_target="tpu_custom_call" | custom-call | tf_op jit(solution)/shard_map/hessian/pallas_call | solution.py:224
  23.1 0.6 %copy.8 = f32[1,16,768]{2,1,0:T(8,128)} copy(f32[1,16,768]{2,1,0:T(8,128)S(1)} %get-tuple-element.2) | data formatting | bytes 98304
  23.7 0.5 %copy.9 = f32[1,16]{1,0:T(1,128)} copy(f32[1,16]{1,0:T(1,128)S(1)} %get-tuple-element.3) | data formatting | bytes 128

commit v4 on v3

--- a/solution.py
+++ b/solution.py
@@ -8,7 +8,7 @@
 from jax.sharding import PartitionSpec as P
 
 MESH = pl.DeviceIdType.MESH
-CHUNKS = 2
+TAIL = 16
 PIECES = 2
 
 
@@ -20,7 +20,7 @@
 
 def kernel(
     n_blk, n_lab, feats, dirs, active, short, hess, curve,
-    slab, group, act, tiles, weights, scaled, acc, from_x, from_z,
+    slab, group, act, tiles, weights, acc, from_x, from_z,
     local_sem, y_send, y_recv, s_send, s_recv, f_send, f_recv,
     g_send, g_recv, h_send, h_recv, x_send, x_recv, z_send, z_recv,
 ):
@@ -28,7 +28,7 @@
     own = dirs.shape[1]
     n_z, n_pair = n_blk // 2, n_lab // 2
     labels = n_blk * own
-    part = rows // CHUNKS
+    cuts = (pl.ds(0, rows // 2), pl.ds(rows // 2, rows // 2 - TAIL), pl.ds(rows - TAIL, TAIL))
     blk, lab = lax.axis_index("blk"), lax.axis_index("lab")
     x, z = lax.rem(blk, 2), lax.div(blk, 2)
     core, pair = lax.rem(lab, 2), lax.div(lab, 2)
@@ -41,9 +41,6 @@
         pltpu.make_async_copy(active, act, local_sem.at[2]),
         pltpu.make_async_copy(short, tiles, local_sem.at[3]),
     ]
-    for copy in local:
-        copy.start()
-
     barrier = pltpu.get_barrier_semaphore()
     for k in range(1, n_z):
         pl.semaphore_signal(
@@ -51,11 +48,14 @@
         )
     pl.semaphore_signal(barrier, inc=1, device_id={"blk": x_peer}, device_id_type=MESH)
     for k in range(1, n_pair):
-        pl.semaphore_signal(
-            barrier, inc=1, device_id={"lab": 2 * lax.rem(pair + k, n_pair) + core}, device_id_type=MESH
-        )
+        for side in range(2):
+            pl.semaphore_signal(
+                barrier, inc=1, device_id={"lab": 2 * lax.rem(pair + k, n_pair) + side}, device_id_type=MESH
+            )
     pl.semaphore_signal(barrier, inc=1, device_id={"lab": core_peer}, device_id_type=MESH)
-    pl.semaphore_wait(barrier, n_z + n_pair)
+    for copy in local:
+        copy.start()
+    pl.semaphore_wait(barrier, n_z + 2 * n_pair - 1)
 
     sent = []
 
@@ -63,13 +63,18 @@
         copy.start()
         sent.append(copy)
 
-    for c in range(CHUNKS):
-        piece = pl.ds(c * part, part)
+    for c, piece in enumerate(cuts):
         for k in range(1, n_pair):
+            to = 2 * lax.rem(pair + k, n_pair)
             go(remote(
                 feats.at[piece], slab.at[pair, core, piece], y_send.at[k - 1, c], y_recv.at[k - 1, c],
-                lab=2 * lax.rem(pair + k, n_pair) + core,
+                lab=to + core,
             ))
+            if c == len(cuts) - 1:
+                go(remote(
+                    feats.at[piece], slab.at[pair, core, piece], f_send.at[k - 1, c], f_recv.at[k - 1, c],
+                    lab=to + 1 - core,
+                ))
     for k in range(1, n_z):
         go(remote(
             dirs.at[0], group.at[x, z], g_send.at[k - 1], g_recv.at[k - 1], blk=2 * lax.rem(z + k, n_z) + x
@@ -88,44 +93,44 @@
             block, offset = divmod(r * row_tile, rows)
             for j in range(label_tile // own):
                 device = t * (label_tile // own) + j
-                slot = (device % 2) * n_z * own + (device // 2) * own
-                weights[block // 2, block % 2, slot:slot + own, offset:offset + row_tile] = tile[j * own:(j + 1) * own]
+                slot = (device // 2) * own
+                weights[block // 2, block % 2, device % 2, slot:slot + own, offset:offset + row_tile] = tile[j * own:(j + 1) * own]
 
     for k in range(1, n_z):
         block = group.at[x, lax.rem(z + n_z - k, n_z)]
         remote(block, block, g_send.at[k - 1], g_recv.at[k - 1], blk=x_peer).wait_recv()
         go(remote(block, block, h_send.at[k], h_recv.at[k], blk=x_peer))
 
-    def pass_on(c):
+    def direct(k, c):
+        block = slab.at[lax.rem(pair + n_pair - k, n_pair), core, cuts[c]]
+        remote(block, block, y_send.at[k - 1, c], y_recv.at[k - 1, c], lab=core_peer).wait_recv()
+        return block
+
+    for c in range(len(cuts) - 1):
         for k in range(1, n_pair):
-            block = slab.at[lax.rem(pair + n_pair - k, n_pair), core, pl.ds(c * part, part)]
-            remote(block, block, y_send.at[k - 1, c], y_recv.at[k - 1, c], lab=core_peer).wait_recv()
+            block = direct(k, c)
             go(remote(block, block, f_send.at[k - 1, c], f_recv.at[k - 1, c], lab=core_peer))
-
-    for c in range(CHUNKS):
-        pass_on(c)
     local[0].wait()
     local[1].wait()
     for k in range(n_z):
         block = group.at[1 - x, lax.rem(z + n_z - k, n_z)]
         remote(block, block, h_send.at[k], h_recv.at[k], blk=x_peer).wait_recv()
 
-    def masked(at, side):
+    def term(vectors, mask, block):
         margins = lax.dot_general(
-            group[...].reshape(labels, depth), slab[at, side],
-            (((1,), (1,)), ((), ())), preferred_element_type=jnp.float32,
+            vectors, block, (((1,), (1,)), ((), ())), preferred_element_type=jnp.float32
         )
-        return (weights[at, side] * margins).astype(jnp.bfloat16)
+        return jnp.dot((mask * margins).astype(jnp.bfloat16), block, preferred_element_type=jnp.float32)
 
     def whole(at, side):
-        return jnp.dot(
-            masked(at, side), slab[at, side], preferred_element_type=jnp.float32
+        return term(
+            group[...].reshape(labels, depth), weights[at, side].reshape(labels, rows), slab[at, side]
         ).reshape(acc.shape)
 
     def arrive(k):
         source = lax.rem(pair + n_pair - k, n_pair)
-        for c in range(CHUNKS):
-            block = slab.at[source, 1 - core, pl.ds(c * part, part)]
+        for c, piece in enumerate(cuts):
+            block = slab.at[source, 1 - core, piece]
             remote(block, block, f_send.at[k - 1, c], f_recv.at[k - 1, c], lab=core_peer).wait_recv()
 
     acc[...] = whole(pair, core)
@@ -136,18 +141,19 @@
         @pl.loop(1, n_pair - 1)
         def _(k):
             source = lax.rem(pair + n_pair - k, n_pair)
+            direct(k, len(cuts) - 1)
             acc[...] += whole(source, core)
             arrive(k)
             acc[...] += whole(source, 1 - core)
 
     last = lax.rem(pair + 1, n_pair)
+    direct(n_pair - 1, len(cuts) - 1)
     acc[...] += whole(last, core)
     arrive(n_pair - 1)
-    scaled[...] = masked(last, 1 - core).reshape(scaled.shape)
 
     def finish(half):
-        acc[half] += jnp.dot(
-            scaled[half], slab[last, 1 - core], preferred_element_type=jnp.float32
+        acc[half] += term(
+            group[half].reshape(labels // 2, depth), weights[last, 1 - core, half], slab[last, 1 - core]
         ).reshape(acc.shape[1:])
 
     finish(1 - x)
@@ -205,15 +211,14 @@
             pltpu.VMEM((2, n_z, own, depth), direction.dtype),
             pltpu.VMEM(active.shape, active.dtype),
             pltpu.VMEM(shortlist.shape[::-1], shortlist.dtype),
-            pltpu.VMEM((n_pair, 2, labels, rows), jnp.float32),
-            pltpu.VMEM((2, n_z * own, rows), jnp.bfloat16),
+            pltpu.VMEM((n_pair, 2, 2, labels // 2, rows), jnp.float32),
             pltpu.VMEM((2, n_z, own, depth), jnp.float32),
             pltpu.VMEM((n_z, own, depth), jnp.float32),
             pltpu.VMEM((n_z - 1, own, depth), jnp.float32),
             dma((4,)),
-            dma((others, CHUNKS)), dma((others, CHUNKS)),
+            dma((others, 3)), dma((others, 3)),
             dma((1,)), dma((1,)),
-            dma((others, CHUNKS)), dma((others, CHUNKS)),
+            dma((others, 3)), dma((others, 3)),
             dma((n_z - 1,)), dma((n_z - 1,)),
             dma((n_z,)), dma((n_z,)),
             dma((n_z, PIECES)), dma((n_z, PIECES)),

time: 24.4 us -> 24.6 us (level)
  no operation moved by 1% of the time
where the time goes in v4:
time: 24.6 us; the launch traced here: 24.5 us
  Pallas kernels  22.7 us (92%)
  local copies, waits for them, and re-layouts  1.13 us (5%)
  between operations  0.64 us (3%)
    pallas_call x1, Pallas kernels, shards(): pl.pallas_call(functools.partial(kernel, n_blk, n_lab), out_shape=(pltpu....  22.7 us
    unnamed x2, local copies, waits for them, and re-layouts  1.13 us

profile of v4, /device:TPU:0, one launch (start us, length us, event | category | flops | bytes accessed | tf_op | source)
XLA Modules:
  0.0 24.5 jit_solution(13172067289192411351)
XLA Ops:
  0.6 22.7 %hessian.1 = (f32[1,16,768]{2,1,0:T(8,128)S(1)}, f32[1,16]{1,0:T(1,128)S(1)}) custom-call(bf16[128,768]{1,0:T(8,128)(2,1)} %feats.1, bf16[1,16,768]{2,1,0:T(8,128)(2,1)} %dirs.1, s32[512,128]{1,0:T(8,128)} %active.1, s32[1,4]{1,0:T(1,128)} %bitcast.1), custom_call_target="tpu_custom_call" | custom-call | tf_op jit(solution)/shard_map/hessian/pallas_call | solution.py:229
  23.3 0.6 %copy.8 = f32[1,16,768]{2,1,0:T(8,128)} copy(f32[1,16,768]{2,1,0:T(8,128)S(1)} %get-tuple-element.2) | data formatting | bytes 98304
  23.9 0.5 %copy.9 = f32[1,16]{1,0:T(1,128)} copy(f32[1,16]{1,0:T(1,128)S(1)} %get-tuple-element.3) | data formatting | bytes 128

commit v5 on v4

--- a/solution.py
+++ b/solution.py
@@ -28,7 +28,7 @@
     own = dirs.shape[1]
     n_z, n_pair = n_blk // 2, n_lab // 2
     labels = n_blk * own
-    cuts = (pl.ds(0, rows // 2), pl.ds(rows // 2, rows // 2 - TAIL), pl.ds(rows - TAIL, TAIL))
+    cuts = (pl.ds(0, rows - TAIL), pl.ds(rows - TAIL, TAIL))
     blk, lab = lax.axis_index("blk"), lax.axis_index("lab")
     x, z = lax.rem(blk, 2), lax.div(blk, 2)
     core, pair = lax.rem(lab, 2), lax.div(lab, 2)
@@ -63,6 +63,11 @@
         copy.start()
         sent.append(copy)
 
+    for k in range(1, n_z):
+        go(remote(
+            dirs.at[0], group.at[x, z], g_send.at[k - 1], g_recv.at[k - 1], blk=2 * lax.rem(z + k, n_z) + x
+        ))
+    go(remote(dirs.at[0], group.at[x, z], h_send.at[0], h_recv.at[0], blk=x_peer))
     for c, piece in enumerate(cuts):
         for k in range(1, n_pair):
             to = 2 * lax.rem(pair + k, n_pair)
@@ -75,11 +80,6 @@
                     feats.at[piece], slab.at[pair, core, piece], f_send.at[k - 1, c], f_recv.at[k - 1, c],
                     lab=to + 1 - core,
                 ))
-    for k in range(1, n_z):
-        go(remote(
-            dirs.at[0], group.at[x, z], g_send.at[k - 1], g_recv.at[k - 1], blk=2 * lax.rem(z + k, n_z) + x
-        ))
-    go(remote(dirs.at[0], group.at[x, z], h_send.at[0], h_recv.at[0], blk=x_peer))
     go(remote(feats, slab.at[pair, core], s_send.at[0], s_recv.at[0], lab=core_peer))
 
     local[2].wait()
@@ -90,11 +90,11 @@
         for t in range(short.shape[0]):
             tile = act[r * row_tile:(r + 1) * row_tile, t * label_tile:(t + 1) * label_tile] * tiles[t:t + 1, r:r + 1]
             tile = tile.astype(jnp.float32).T
-            block, offset = divmod(r * row_tile, rows)
+            at_pair, offset = divmod(r * row_tile, 2 * rows)
             for j in range(label_tile // own):
                 device = t * (label_tile // own) + j
                 slot = (device // 2) * own
-                weights[block // 2, block % 2, device % 2, slot:slot + own, offset:offset + row_tile] = tile[j * own:(j + 1) * own]
+                weights[at_pair, device % 2, slot:slot + own, offset:offset + row_tile] = tile[j * own:(j + 1) * own]
 
     for k in range(1, n_z):
         block = group.at[x, lax.rem(z + n_z - k, n_z)]
@@ -122,38 +122,33 @@
         )
         return jnp.dot((mask * margins).astype(jnp.bfloat16), block, preferred_element_type=jnp.float32)
 
-    def whole(at, side):
+    def whole(at):
         return term(
-            group[...].reshape(labels, depth), weights[at, side].reshape(labels, rows), slab[at, side]
+            group[...].reshape(labels, depth), weights[at].reshape(labels, 2 * rows),
+            slab[at].reshape(2 * rows, depth),
         ).reshape(acc.shape)
 
     def arrive(k):
         source = lax.rem(pair + n_pair - k, n_pair)
+        direct(k, len(cuts) - 1)
         for c, piece in enumerate(cuts):
             block = slab.at[source, 1 - core, piece]
             remote(block, block, f_send.at[k - 1, c], f_recv.at[k - 1, c], lab=core_peer).wait_recv()
-
-    acc[...] = whole(pair, core)
+        return source
+
     other = slab.at[pair, 1 - core]
     remote(other, other, s_send.at[0], s_recv.at[0], lab=core_peer).wait_recv()
-    acc[...] += whole(pair, 1 - core)
+    acc[...] = whole(pair)
     if n_pair > 2:
         @pl.loop(1, n_pair - 1)
         def _(k):
-            source = lax.rem(pair + n_pair - k, n_pair)
-            direct(k, len(cuts) - 1)
-            acc[...] += whole(source, core)
-            arrive(k)
-            acc[...] += whole(source, 1 - core)
-
-    last = lax.rem(pair + 1, n_pair)
-    direct(n_pair - 1, len(cuts) - 1)
-    acc[...] += whole(last, core)
-    arrive(n_pair - 1)
+            acc[...] += whole(arrive(k))
+
+    last = arrive(n_pair - 1)
 
     def finish(half):
         acc[half] += term(
-            group[half].reshape(labels // 2, depth), weights[last, 1 - core, half], slab[last, 1 - core]
+            group[half].reshape(labels // 2, depth), weights[last, half], slab[last].reshape(2 * rows, depth)
         ).reshape(acc.shape[1:])
 
     finish(1 - x)
@@ -211,14 +206,14 @@
             pltpu.VMEM((2, n_z, own, depth), direction.dtype),
             pltpu.VMEM(active.shape, active.dtype),
             pltpu.VMEM(shortlist.shape[::-1], shortlist.dtype),
-            pltpu.VMEM((n_pair, 2, 2, labels // 2, rows), jnp.float32),
+            pltpu.VMEM((n_pair, 2, labels // 2, 2 * rows), jnp.float32),
             pltpu.VMEM((2, n_z, own, depth), jnp.float32),
             pltpu.VMEM((n_z, own, depth), jnp.float32),
             pltpu.VMEM((n_z - 1, own, depth), jnp.float32),
             dma((4,)),
-            dma((others, 3)), dma((others, 3)),
+            dma((others, 2)), dma((others, 2)),
             dma((1,)), dma((1,)),
-            dma((others, 3)), dma((others, 3)),
+            dma((others, 2)), dma((others, 2)),
             dma((n_z - 1,)), dma((n_z - 1,)),
             dma((n_z,)), dma((n_z,)),
             dma((n_z, PIECES)), dma((n_z, PIECES)),

time: 24.6 us -> 24.4 us (level)
  no operation moved by 1% of the time
where the time goes in v5:
time: 24.4 us; the launch traced here: 24.3 us
  Pallas kernels  22.5 us (92%)
  local copies, waits for them, and re-layouts  1.13 us (5%)
  between operations  0.64 us (3%)
    pallas_call x1, Pallas kernels, shards(): pl.pallas_call(functools.partial(kernel, n_blk, n_lab), out_shape=(pltpu....  22.5 us
    unnamed x2, local copies, waits for them, and re-layouts  1.13 us

profile of v5, /device:TPU:0, one launch (start us, length us, event | category | flops | bytes accessed | tf_op | source)
XLA Modules:
  0.0 24.3 jit_solution(1074295656186678572)
XLA Ops:
  0.6 22.5 %hessian.1 = (f32[1,16,768]{2,1,0:T(8,128)S(1)}, f32[1,16]{1,0:T(1,128)S(1)}) custom-call(bf16[128,768]{1,0:T(8,128)(2,1)} %feats.1, bf16[1,16,768]{2,1,0:T(8,128)(2,1)} %dirs.1, s32[512,128]{1,0:T(8,128)} %active.1, s32[1,4]{1,0:T(1,128)} %bitcast.1), custom_call_target="tpu_custom_call" | custom-call | tf_op jit(solution)/shard_map/hessian/pallas_call | solution.py:224
  23.2 0.6 %copy.8 = f32[1,16,768]{2,1,0:T(8,128)} copy(f32[1,16,768]{2,1,0:T(8,128)S(1)} %get-tuple-element.2) | data formatting | bytes 98304
  23.8 0.5 %copy.9 = f32[1,16]{1,0:T(1,128)} copy(f32[1,16]{1,0:T(1,128)S(1)} %get-tuple-element.3) | data formatting | bytes 128

commit v6 on v5

--- a/solution.py
+++ b/solution.py
@@ -10,6 +10,7 @@
 MESH = pl.DeviceIdType.MESH
 TAIL = 16
 PIECES = 2
+STRAIGHT = 128
 
 
 def remote(src, dst, send, recv, **where):
@@ -20,9 +21,10 @@
 
 def kernel(
     n_blk, n_lab, feats, dirs, active, short, hess, curve,
-    slab, group, act, tiles, weights, acc, from_x, from_z,
+    slab, group, act, tiles, weights, acc, from_x, from_z, from_far,
     local_sem, y_send, y_recv, s_send, s_recv, f_send, f_recv,
     g_send, g_recv, h_send, h_recv, x_send, x_recv, z_send, z_recv,
+    d_send, d_recv,
 ):
     rows, depth = feats.shape
     own = dirs.shape[1]
@@ -42,11 +44,8 @@
         pltpu.make_async_copy(short, tiles, local_sem.at[3]),
     ]
     barrier = pltpu.get_barrier_semaphore()
-    for k in range(1, n_z):
-        pl.semaphore_signal(
-            barrier, inc=1, device_id={"blk": 2 * lax.rem(z + k, n_z) + x}, device_id_type=MESH
-        )
-    pl.semaphore_signal(barrier, inc=1, device_id={"blk": x_peer}, device_id_type=MESH)
+    for k in range(1, n_blk):
+        pl.semaphore_signal(barrier, inc=1, device_id={"blk": lax.rem(blk + k, n_blk)}, device_id_type=MESH)
     for k in range(1, n_pair):
         for side in range(2):
             pl.semaphore_signal(
@@ -55,7 +54,7 @@
     pl.semaphore_signal(barrier, inc=1, device_id={"lab": core_peer}, device_id_type=MESH)
     for copy in local:
         copy.start()
-    pl.semaphore_wait(barrier, n_z + 2 * n_pair - 1)
+    pl.semaphore_wait(barrier, n_blk - 1 + 2 * n_pair - 1)
 
     sent = []
 
@@ -151,35 +150,57 @@
             group[half].reshape(labels // 2, depth), weights[last, half], slab[last].reshape(2 * rows, depth)
         ).reshape(acc.shape[1:])
 
+    step = own // PIECES
+    wide = pl.ds(STRAIGHT, depth - STRAIGHT)
+    narrow = pl.ds(0, STRAIGHT)
+
+    def straight(half, at):
+        for i in range(n_z - 1):
+            to = lax.rem(z + 1 + i, n_z)
+            go(remote(
+                acc.at[half, to, :, narrow], from_far.at[i, x], d_send.at[i, at], d_recv.at[i, x],
+                blk=2 * to + half,
+            ))
+
+    def pieces(i):
+        for c in range(PIECES):
+            yield c, (pl.ds(c * step, step), wide if i < n_z - 1 else pl.ds(0, depth))
+
     finish(1 - x)
-    step = own // PIECES
     for i in range(n_z):
         to = lax.rem(z + 1 + i, n_z)
-        for c in range(PIECES):
-            piece = pl.ds(c * step, step)
+        for c, piece in pieces(i):
             go(remote(
-                acc.at[1 - x, to, piece], from_x.at[to, piece], x_send.at[i, c], x_recv.at[i, c], blk=x_peer
+                acc.at[(1 - x, to, *piece)], from_x.at[(to, *piece)], x_send.at[i, c], x_recv.at[i, c], blk=x_peer
             ))
+        if i == 0:
+            straight(1 - x, 1)
     finish(x)
+    straight(x, 0)
     for i in range(n_z):
         to = lax.rem(z + 1 + i, n_z)
-        for c in range(PIECES):
-            piece = pl.ds(c * step, step)
-            block = from_x.at[to, piece]
+        for c, piece in pieces(i):
+            block = from_x.at[(to, *piece)]
             remote(block, block, x_send.at[i, c], x_recv.at[i, c], blk=x_peer).wait_recv()
-            acc[x, to, piece] += from_x[to, piece]
+            acc[(x, to, *piece)] += from_x[(to, *piece)]
             if i < n_z - 1:
                 go(remote(
-                    acc.at[x, to, piece], from_z.at[i, piece], z_send.at[i, c], z_recv.at[i, c], blk=2 * to + x
+                    acc.at[(x, to, *piece)], from_z.at[(i, *piece)], z_send.at[i, c], z_recv.at[i, c],
+                    blk=2 * to + x,
                 ))
 
     vectors = group[x, z].astype(jnp.float32)
+    for i in range(n_z - 1):
+        for side in range(2):
+            block = from_far.at[i, side]
+            remote(block, block, d_send.at[i, side], d_recv.at[i, side], blk=x_peer).wait_recv()
+        acc[x, z, :, narrow] += from_far[i, 0] + from_far[i, 1]
+    for i in range(n_z - 1):
+        for c, piece in pieces(i):
+            block = from_z.at[(i, *piece)]
+            remote(block, block, z_send.at[i, c], z_recv.at[i, c], blk=x_peer).wait_recv()
+        acc[x, z, :, wide] += from_z[i, :, wide]
     total = acc[x, z]
-    for i in range(n_z - 1):
-        for c in range(PIECES):
-            block = from_z.at[i, pl.ds(c * step, step)]
-            remote(block, block, z_send.at[i, c], z_recv.at[i, c], blk=x_peer).wait_recv()
-        total += from_z[i]
     product = vectors + total
     hess[0] = product
     column = jnp.sum(vectors * product, axis=1, keepdims=True) / depth
@@ -210,6 +231,7 @@
             pltpu.VMEM((2, n_z, own, depth), jnp.float32),
             pltpu.VMEM((n_z, own, depth), jnp.float32),
             pltpu.VMEM((n_z - 1, own, depth), jnp.float32),
+            pltpu.VMEM((n_z - 1, 2, own, STRAIGHT), jnp.float32),
             dma((4,)),
             dma((others, 2)), dma((others, 2)),
             dma((1,)), dma((1,)),
@@ -218,6 +240,7 @@
             dma((n_z,)), dma((n_z,)),
             dma((n_z, PIECES)), dma((n_z, PIECES)),
             dma((n_z - 1, PIECES)), dma((n_z - 1, PIECES)),
+            dma((n_z - 1, 2)), dma((n_z - 1, 2)),
         ]
         hbm = pl.BlockSpec(memory_space=pltpu.HBM)
         vmem = pl.BlockSpec(memory_space=pltpu.VMEM)

time: 24.4 us -> 24.8 us (1.016)
  Pallas kernels: 22.5 us -> 22.9 us
    pallas_call x1, Pallas kernels: 22.5 us -> 22.9 us  [shards(): pl.pallas_call(functools.partial(kernel, n_blk, n_lab), out_shape=(pltpu....]
where the time goes in v6:
time: 24.8 us; the launch traced here: 24.7 us
  Pallas kernels  22.9 us (92%)
  local copies, waits for them, and re-layouts  1.13 us (5%)
  between operations  0.64 us (3%)
    pallas_call x1, Pallas kernels, shards(): pl.pallas_call(functools.partial(kernel, n_blk, n_lab), out_shape=(pltpu....  22.9 us
    unnamed x2, local copies, waits for them, and re-layouts  1.13 us

profile of v6, /device:TPU:0, one launch (start us, length us, event | category | flops | bytes accessed | tf_op | source)
XLA Modules:
  0.0 24.7 jit_solution(4989814253329038967)
XLA Ops:
  0.6 22.9 %hessian.1 = (f32[1,16,768]{2,1,0:T(8,128)S(1)}, f32[1,16]{1,0:T(1,128)S(1)}) custom-call(bf16[128,768]{1,0:T(8,128)(2,1)} %feats.1, bf16[1,16,768]{2,1,0:T(8,128)(2,1)} %dirs.1, s32[512,128]{1,0:T(8,128)} %active.1, s32[1,4]{1,0:T(1,128)} %bitcast.1), custom_call_target="tpu_custom_call" | custom-call | tf_op jit(solution)/shard_map/hessian/pallas_call | solution.py:247
  23.5 0.6 %copy.8 = f32[1,16,768]{2,1,0:T(8,128)} copy(f32[1,16,768]{2,1,0:T(8,128)S(1)} %get-tuple-element.2) | data formatting | bytes 98304
  24.2 0.5 %copy.9 = f32[1,16]{1,0:T(1,128)} copy(f32[1,16]{1,0:T(1,128)S(1)} %get-tuple-element.3) | data formatting | bytes 128

commit v7 on v5

--- a/solution.py
+++ b/solution.py
@@ -151,10 +151,18 @@
             group[half].reshape(labels // 2, depth), weights[last, half], slab[last].reshape(2 * rows, depth)
         ).reshape(acc.shape[1:])
 
+    def partner(i):
+        to, bit = z, 1
+        while bit < n_z:
+            if (n_z - 1 - i) & bit:
+                to = to + bit * (1 - 2 * lax.rem(lax.div(z, bit), 2))
+            bit *= 2
+        return to
+
     finish(1 - x)
     step = own // PIECES
     for i in range(n_z):
-        to = lax.rem(z + 1 + i, n_z)
+        to = partner(i)
         for c in range(PIECES):
             piece = pl.ds(c * step, step)
             go(remote(
@@ -162,7 +170,7 @@
             ))
     finish(x)
     for i in range(n_z):
-        to = lax.rem(z + 1 + i, n_z)
+        to = partner(i)
         for c in range(PIECES):
             piece = pl.ds(c * step, step)
             block = from_x.at[to, piece]

time: 24.4 us -> 24.5 us (level)
  no operation moved by 1% of the time
where the time goes in v7:
time: 24.5 us; the launch traced here: 24.3 us
  Pallas kernels  22.5 us (92%)
  local copies, waits for them, and re-layouts  1.13 us (5%)
  between operations  0.64 us (3%)
    pallas_call x1, Pallas kernels, shards(): pl.pallas_call(functools.partial(kernel, n_blk, n_lab), out_shape=(pltpu....  22.5 us
    unnamed x2, local copies, waits for them, and re-layouts  1.13 us

profile of v7, /device:TPU:0, one launch (start us, length us, event | category | flops | bytes accessed | tf_op | source)
XLA Modules:
  0.0 24.3 jit_solution(12774009962701644251)
XLA Ops:
  0.6 22.5 %hessian.1 = (f32[1,16,768]{2,1,0:T(8,128)S(1)}, f32[1,16]{1,0:T(1,128)S(1)}) custom-call(bf16[128,768]{1,0:T(8,128)(2,1)} %feats.1, bf16[1,16,768]{2,1,0:T(8,128)(2,1)} %dirs.1, s32[512,128]{1,0:T(8,128)} %active.1, s32[1,4]{1,0:T(1,128)} %bitcast.1), custom_call_target="tpu_custom_call" | custom-call | tf_op jit(solution)/shard_map/hessian/pallas_call | solution.py:232
  23.2 0.6 %copy.8 = f32[1,16,768]{2,1,0:T(8,128)} copy(f32[1,16,768]{2,1,0:T(8,128)S(1)} %get-tuple-element.2) | data formatting | bytes 98304
  23.8 0.5 %copy.9 = f32[1,16]{1,0:T(1,128)} copy(f32[1,16]{1,0:T(1,128)S(1)} %get-tuple-element.3) | data formatting | bytes 128
